TPU v7x, 32 devices: a whole 2x2x4 slice. The times are simulated.
32 devices in a mesh: group: 2 (over x), frame: 16 (over z, y, core).
Axes of the slice: x: 2, y: 2, z: 4, core: 2. Of those that a mesh axis runs over, the one named last changes fastest.
Arguments:
- queries: bfloat16 [10240, 5120], P(('group', 'frame')), parts along dimension 0, may hold values from -33 to 33
- keys: bfloat16 [10240, 5120], P(('group', 'frame')), parts along dimension 0, may hold values from -33 to 33
- values: bfloat16 [10240, 5120], P(('group', 'frame')), parts along dimension 0, may hold values from -6 to 6
- labels: int32 [80], P('group'), parts along dimension 0, may hold values from 0 to 1, as said below
- band: int32 [80], P('group'), parts along dimension 0, may hold values from 2 to 4
Outputs:
- attended: bfloat16 [10240, 5120], P(('group', 'frame')), parts along dimension 0
There are 2 independent parts, one for each index of `group`. A program takes and returns all parts, laid end to end along the dimension named above; each array names one. Nothing has to cross between parts.
Inputs may be any that keep to these rules, and one draw needn't show every extreme that they name: `labels`: exactly 10 of the 40 heads carry 1, the others 0.
All inputs are finite; a program needn't handle non-finite values.
Results may differ from a plain program's by a relative error of at most 0.0049.
Values may be sent and summed in bfloat16 or wider, within the bound.
No kernel may reach another device: no remote copies, remote signals or barrier semaphores. Data moves between devices by JAX's collectives and lax.ppermute only.
A program may use at most 128 MiB of HBM per device.

v0:
```python
import math

import jax
import jax.numpy as jnp
from jax import lax
from jax.sharding import PartitionSpec as P

TEMP_HEADS = 10


def from_partner(block, axis, bit):
    count = lax.axis_size(axis)
    route = []
    for low in range(count):
        high = low | 1 << bit
        if high != low and high < count:
            route += [(low, high), (high, low)]
    return lax.ppermute(block, axis, route)


def softmax_rounded(scores):
    peak = jnp.max(scores, axis=-1, keepdims=True)
    weights = jnp.exp(scores - peak)
    return (weights / jnp.sum(weights, axis=-1, keepdims=True)).astype(jnp.bfloat16)


def block_heads(count):
    for candidate in (6, 5, 4, 3, 2):
        if count % candidate == 0:
            return candidate
    return 1


def attend_spatial(query_part, key_all, value_all):
    head_total = query_part.shape[1]
    step_heads = block_heads(head_total)
    scale = 1.0 / math.sqrt(query_part.shape[2])

    def one_block(block_number, result):
        start = block_number * step_heads
        query_block = lax.dynamic_slice_in_dim(query_part, start, step_heads, 1)
        key_block = lax.dynamic_slice_in_dim(key_all, start, step_heads, 1)
        value_block = lax.dynamic_slice_in_dim(value_all, start, step_heads, 1)
        scores = (
            jnp.einsum("rhd,khd->hrk", query_block, key_block, preferred_element_type=jnp.float32)
            * scale
        )
        weights = softmax_rounded(scores)
        output_block = jnp.einsum(
            "hrk,khd->rhd", weights, value_block, preferred_element_type=jnp.float32
        ).astype(jnp.bfloat16)
        return lax.dynamic_update_slice_in_dim(result, output_block, start, 1)

    initial = jnp.zeros(query_part.shape, jnp.bfloat16)
    return lax.fori_loop(0, head_total // step_heads, one_block, initial)


def attend_columns(query_part, key_part, value_part, head_band):
    query_cols, key_cols, value_cols = (
        lax.all_to_all(query_part[None], "frame", split_axis=1, concat_axis=0, tiled=True),
        lax.all_to_all(key_part[None], "frame", split_axis=1, concat_axis=0, tiled=True),
        lax.all_to_all(value_part[None], "frame", split_axis=1, concat_axis=0, tiled=True),
    )
    sources, pixels, head_part, head_size = query_cols.shape
    frames = sources // 2
    scale = 1.0 / math.sqrt(head_size)
    grid_shape = (frames, 2, pixels, head_part, head_size)
    scores = (
        jnp.einsum(
            "fapnd,gapnd->apnfg",
            query_cols.reshape(grid_shape),
            key_cols.reshape(grid_shape),
            preferred_element_type=jnp.float32,
        )
        * scale
    )
    frame_ids = jnp.arange(frames, dtype=jnp.int32)
    distance = jnp.abs(frame_ids[:, None] - frame_ids[None, :])
    keep = distance[None, :, :] <= head_band[:, None, None]
    scores = jnp.where(keep, scores, jnp.float32(-1e30))
    weights = softmax_rounded(scores)
    output = jnp.einsum(
        "apnfg,gapnd->fapnd",
        weights,
        value_cols.reshape(grid_shape),
        preferred_element_type=jnp.float32,
    ).astype(jnp.bfloat16)
    output = output.reshape(sources, pixels, head_part, head_size)
    returned = lax.all_to_all(output, "frame", split_axis=0, concat_axis=1, tiled=True)
    return returned[0]


def shards(queries, keys, values, labels, band):
    row_count = queries.shape[0]
    head_count = labels.shape[0]
    head_size = queries.shape[1] // head_count
    query_heads = queries.reshape(row_count, head_count, head_size)
    key_heads = keys.reshape(row_count, head_count, head_size)
    value_heads = values.reshape(row_count, head_count, head_size)
    spatial_count = head_count - TEMP_HEADS
    ordering = jnp.argsort(labels, stable=True)
    spatial_index = ordering[:spatial_count]
    temporal_index = ordering[spatial_count:]
    inverse = jnp.argsort(ordering, stable=True)
    query_spatial = jnp.take(query_heads, spatial_index, axis=1)
    key_spatial = jnp.take(key_heads, spatial_index, axis=1)
    value_spatial = jnp.take(value_heads, spatial_index, axis=1)
    temporal_band = jnp.take(band, temporal_index)
    temporal = attend_columns(
        jnp.take(query_heads, temporal_index, axis=1),
        jnp.take(key_heads, temporal_index, axis=1),
        jnp.take(value_heads, temporal_index, axis=1),
        temporal_band,
    )
    parity = lax.axis_index("frame") % 2
    half = spatial_count // 2
    mine_start = parity * half
    other_start = (1 - parity) * half
    query_mine = lax.dynamic_slice_in_dim(query_spatial, mine_start, half, 1)
    key_mine = lax.dynamic_slice_in_dim(key_spatial, mine_start, half, 1)
    value_mine = lax.dynamic_slice_in_dim(value_spatial, mine_start, half, 1)
    query_other = lax.dynamic_slice_in_dim(query_spatial, other_start, half, 1)
    key_other = lax.dynamic_slice_in_dim(key_spatial, other_start, half, 1)
    value_other = lax.dynamic_slice_in_dim(value_spatial, other_start, half, 1)
    query_got, key_got, value_got = from_partner((query_other, key_other, value_other), "frame", 0)

    def whole_frame(own, got):
        return jnp.where(
            parity == 0, jnp.concatenate([own, got], axis=0), jnp.concatenate([got, own], axis=0)
        )

    frame_out = attend_spatial(
        whole_frame(query_mine, query_got),
        whole_frame(key_mine, key_got),
        whole_frame(value_mine, value_got),
    )
    own_rows = lax.dynamic_slice_in_dim(frame_out, parity * row_count, row_count, 0)
    other_rows = lax.dynamic_slice_in_dim(frame_out, (1 - parity) * row_count, row_count, 0)
    returned = from_partner(other_rows, "frame", 0)
    spatial = jnp.where(
        parity == 0,
        jnp.concatenate([own_rows, returned], axis=1),
        jnp.concatenate([returned, own_rows], axis=1),
    )
    combined = jnp.take(jnp.concatenate([spatial, temporal], axis=1), inverse, axis=1)
    return combined.reshape(row_count, head_count * head_size)


def solution(mesh):
    placed = (
        P(("group", "frame"), None),
        P(("group", "frame"), None),
        P(("group", "frame"), None),
        P("group"),
        P("group"),
    )
    return jax.shard_map(
        shards, mesh=mesh, in_specs=placed, out_specs=P(("group", "frame"), None), check_vma=False
    )
```

profile of v0, /device:TPU:0, one launch (start us, length us, event | category | flops | bytes accessed | tf_op | source)
XLA Modules:
  0.0 211.7 jit_solution(6797831736654225508)
XLA Ops:
  0.0 1.9 copy-done
  1.9 2.6 %copy_bitcast_fusion.1 = bf16[320,40,128]{2,0,1:T(8,128)(2,1)} fusion(bf16[320,5120]{1,0:T(8,128)(2,1)S(1)} %copy-done), kind=kLoop, calls=%fused_computation.30 | loop fusion | bytes 6553600 | tf_op jit(solution)/shard_map/reshape | solution.py:97
  4.6 2.0 sort.31
  6.7 4.7 %copy_bitcast_fusion = bf16[320,40,128]{2,0,1:T(8,128)(2,1)} fusion(bf16[320,5120]{1,0:T(8,128)(2,1)} %param.12), kind=kLoop, calls=%fused_computation.29 | loop fusion | bytes 6553600 | tf_op jit(solution)/shard_map/reshape | solution.py:98
  11.3 1.6 gather_fusion.6
  13.0 3.5 %gather_fusion.7 = bf16[10,320,128]{2,1,0:T(8,128)(2,1)} fusion(bf16[320,40,128]{2,0,1:T(8,128)(2,1)} %copy_bitcast_fusion, s32[1024]{0:T(1024)S(1)} %pad_clamp_fusion.1), kind=kCustom, calls=%fused_computation.5.clone | custom fusion | bytes 1638440 | tf_op jit(solution)/shard_map/jit(_take)/gather | solution.py:111
  16.5 4.5 %copy_bitcast_fusion.2 = bf16[320,40,128]{2,0,1:T(8,128)(2,1)} fusion(bf16[320,5120]{1,0:T(8,128)(2,1)} %param.13), kind=kLoop, calls=%fused_computation.31 | loop fusion | bytes 6553600 | tf_op jit(solution)/shard_map/reshape | solution.py:99
  21.0 3.5 %gather_fusion.5 = bf16[10,320,128]{2,1,0:T(8,128)(2,1)} fusion(bf16[320,40,128]{2,0,1:T(8,128)(2,1)} %copy_bitcast_fusion.2, s32[1024]{0:T(1024)S(1)} %pad_clamp_fusion.1), kind=kCustom, calls=%fused_computation.1.clone | custom fusion | bytes 1638440 | tf_op jit(solution)/shard_map/jit(_take)/gather | solution.py:112
  24.6 3.1 %select_bitcast_fusion.4 = (bf16[1,320,10,128]{3,1,2,0:T(8,128)(2,1)}, bf16[1,320,10,128]{3,1,2,0:T(8,128)(2,1)S(1)}, bf16[1,320,10,128]{3,1,2,0:T(8,128)(2,1)}) fusion(bf16[10,320,128]{2,1,0:T(8,128)(2,1)} %gather_fusion.6, pred[10]{0:T(512)(128)(4,1)S(1)} %get-tuple-element.148, bf16[10,320,128]{2,1,0:T(8,128)(2,1)} %gather_fusion.7, ...), kind=kLoop, calls=%fused_computation.50 | loop fusion | flops 1228800 | bytes 4915210 | tf_op jit(solution)/shard_map/broadcast_in_dim | solution.py:60
  27.7 1.7 copy.97
  29.4 7.4 %all-to-all-start.2 = ((bf16[1,320,10,128]{3,2,0,1:T(8,128)(2,1)}), bf16[1,320,10,128]{3,2,0,1:T(8,128)(2,1)}, u32[]{:S(2)}, u32[]{:S(2)}) async-start(bf16[1,320,10,128]{3,2,0,1:T(8,128)(2,1)} %copy.97), calls=%async_computation.2 | async-start | bytes 2621440 | tf_op jit(solution)/shard_map/all_to_all | solution.py:61
  36.9 4.3 %gather_fusion.4 = bf16[30,320,128]{2,1,0:T(8,128)(2,1)} fusion(bf16[320,40,128]{2,0,1:T(8,128)(2,1)} %copy_bitcast_fusion, s32[1024]{0:T(1024)S(1)} %pad_clamp_fusion.2), kind=kCustom, calls=%fused_computation.3.clone | custom fusion | bytes 4915320 | tf_op jit(solution)/shard_map/jit(_take)/gather | solution.py:106
  41.2 2.3 %gather_fusion.3 = bf16[30,320,128]{2,1,0:T(8,128)(2,1)} fusion(bf16[320,40,128]{2,0,1:T(8,128)(2,1)S(1)} %copy-done.4, s32[1024]{0:T(1024)S(1)} %pad_clamp_fusion.2), kind=kCustom, calls=%fused_computation.2.clone | custom fusion | bytes 4915320 | tf_op jit(solution)/shard_map/jit(_take)/gather | solution.py:105
  43.5 4.4 %gather_fusion.2 = bf16[30,320,128]{2,1,0:T(8,128)(2,1)} fusion(bf16[320,40,128]{2,0,1:T(8,128)(2,1)} %copy_bitcast_fusion.2, s32[1024]{0:T(1024)S(1)} %pad_clamp_fusion.2), kind=kCustom, calls=%fused_computation.clone | custom fusion | bytes 4915320 | tf_op jit(solution)/shard_map/jit(_take)/gather | solution.py:107
  47.9 4.6 %select_bitcast_fusion = (bf16[320,30,128]{2,0,1:T(8,128)(2,1)}, bf16[320,30,128]{2,0,1:T(8,128)(2,1)S(1)}, bf16[320,30,128]{2,0,1:T(8,128)(2,1)S(1)}) fusion(bf16[30,320,128]{2,1,0:T(8,128)(2,1)S(1)} %copy-done.5, pred[30]{0:T(512)(128)(4,1)S(1)} %get-tuple-element.146, bf16[30,320,128]{2,1,0:T(8,128)(2,1)} %gather_fusion.3, ...), kind=kLoop, calls=%fused_computation.37 | loop fusion | flops 3686400 | bytes 14745630 | tf_op jit(solution)/shard_map/jit(_take)/select_n | solution.py:106
  54.5 1.6 constant_dynamic-slice_fusion.5
  56.2 1.7 copy.94
  57.9 6.4 %all-to-all-done.2 = bf16[1,320,10,128]{3,2,0,1:T(8,128)(2,1)} async-done(((bf16[1,320,10,128]{3,2,0,1:T(8,128)(2,1)}), bf16[1,320,10,128]{3,2,0,1:T(8,128)(2,1)}, u32[]{:S(2)}, u32[]{:S(2)}) %all-to-all-start.2) | async-done | bytes 819232 | tf_op jit(solution)/shard_map/all_to_all | solution.py:61
  64.3 8.1 %all-to-all-start.1 = ((bf16[1,320,10,128]{3,2,0,1:T(8,128)(2,1)}), bf16[1,320,10,128]{3,2,0,1:T(8,128)(2,1)}, u32[]{:S(2)}, u32[]{:S(2)}) async-start(bf16[1,320,10,128]{3,2,0,1:T(8,128)(2,1)} %copy.94), calls=%async_computation.1 | async-start | bytes 2621440 | tf_op jit(solution)/shard_map/all_to_all | solution.py:60
  72.4 1.6 constant_dynamic-slice_fusion.3
  74.4 2.8 %copy.91 = bf16[1,320,10,128]{3,2,0,1:T(8,128)(2,1)} copy(bf16[1,320,10,128]{3,1,2,0:T(8,128)(2,1)} %get-tuple-element.163) | data formatting | bytes 1638400 | tf_op jit(solution)/shard_map/broadcast_in_dim | solution.py:62
  78.0 4.0 %maximum_select_fusion = bf16[640,15,128]{2,0,1:T(8,128)(2,1)} fusion(bf16[320,15,128]{2,0,1:T(8,128)(2,1)} %collective-permute-done, bf16[320,15,128]{2,0,1:T(8,128)(2,1)S(1)} %copy-done.8, pred[]{:T(512)S(6)} %eq.4), kind=kLoop, calls=%fused_computation.33 | loop fusion | flops 11059200 | bytes 4915201 | tf_op jit(solution)/shard_map/jit(_where)/select_n | solution.py:128
  82.0 4.0 %maximum_select_fusion.1 = bf16[640,15,128]{2,0,1:T(8,128)(2,1)} fusion(bf16[320,15,128]{2,0,1:T(8,128)(2,1)} %collective-permute-done.1, bf16[320,15,128]{2,0,1:T(8,128)(2,1)S(1)} %copy-done.9, pred[]{:T(512)S(6)} %eq.4), kind=kLoop, calls=%fused_computation.34 | loop fusion | flops 11059200 | bytes 4915201 | tf_op jit(solution)/shard_map/jit(_where)/select_n | solution.py:128
  86.0 3.8 %maximum_select_fusion.2 = bf16[640,15,128]{2,0,1:T(8,128)(2,1)} fusion(bf16[320,15,128]{2,0,1:T(8,128)(2,1)} %collective-permute-done.2, bf16[320,15,128]{2,0,1:T(8,128)(2,1)S(1)} %copy-done.10, pred[]{:T(512)S(6)} %eq.4), kind=kLoop, calls=%fused_computation.35 | loop fusion | flops 11059200 | bytes 4915201 | tf_op jit(solution)/shard_map/jit(_where)/select_n | solution.py:128
  89.8 10.1 %all-to-all-done.1 = bf16[1,320,10,128]{3,2,0,1:T(8,128)(2,1)} async-done(((bf16[1,320,10,128]{3,2,0,1:T(8,128)(2,1)}), bf16[1,320,10,128]{3,2,0,1:T(8,128)(2,1)}, u32[]{:S(2)}, u32[]{:S(2)}) %all-to-all-start.1) | async-done | bytes 819232 | tf_op jit(solution)/shard_map/all_to_all | solution.py:60
  99.9 8.0 %all-to-all-start = ((bf16[1,320,10,128]{3,2,0,1:T(8,128)(2,1)}), bf16[1,320,10,128]{3,2,0,1:T(8,128)(2,1)S(1)}, u32[]{:S(2)}, u32[]{:S(2)}) async-start(bf16[1,320,10,128]{3,2,0,1:T(8,128)(2,1)} %copy.91), calls=%async_computation | async-start | bytes 2621440 | tf_op jit(solution)/shard_map/all_to_all | solution.py:62
  107.9 1.9 broadcast_in_dim.73.clone
  109.8 50.4 %while.13 = (s32[]{:T(128)}, bf16[640,15,128]{2,0,1:T(8,128)(2,1)}, bf16[640,15,128]{2,0,1:T(8,128)(2,1)}, bf16[640,15,128]{2,0,1:T(8,128)(2,1)}, bf16[640,15,12...) while((s32[]{:T(128)}, bf16[640,15,128]{2,0,1:T(8,128)(2,1)}, ...), condition=%wide.region_5.7_spmd, body=%wide.region_2.6_spmd.sunk | while | flops 1067422080 | bytes 72116400 | solution.py:55
  109.8 2.6 %fusion.48 = f32[5,640,640]{1,2,0:T(8,128)S(1)} fusion(bf16[640,15,128]{2,0,1:T(8,128)(2,1)} %get-tuple-element.219, s32[]{:T(128)S(6)} %select_n.164, bf16[640,15,128]{2,0,1:T(8,128)(2,1)} %get-tuple-element.218), kind=kOutput, calls=%fused_computation.17.clone.1 | convolution fusion | flops 524288000 | bytes 9831424 | tf_op jit(solution)/shard_map/while/body/eval_jaxpr/rhd,khd->hrk/dot_general | solution.py:45
  112.4 2.1 %fusion.49 = f32[5,640]{1,0:T(8,128)S(1)} fusion(f32[5,640,640]{1,2,0:T(8,128)S(1)} %fusion.48), kind=kOutput, calls=%fused_computation.73.clone.1 | output fusion | flops 8192639 | bytes 8204800 | tf_op jit(solution)/shard_map/while/body/eval_jaxpr/sub | solution.py:23
  115.6 8.7 %fusion.50 = bf16[640,5,128]{0,2,1:T(8,128)(2,1)S(1)} fusion(f32[5,640]{1,0:T(8,128)S(1)} %fusion.49, bf16[640,15,128]{2,0,1:T(8,128)(2,1)} %get-tuple-element.217, s32[]{:T(128)S(6)} %select_n.164, f32[5,640,640]{1,2,0:T(8,128)} %copy-done.3), kind=kOutput, calls=%fused_computation.16.clone.1 | convolution fusion | flops 534941440 | bytes 18035204 | tf_op jit(solution)/shard_map/while/body/eval_jaxpr/hrk,khd->rhd/dot_general | solution.py:49
  126.6 2.6 %fusion.48 = f32[5,640,640]{1,2,0:T(8,128)S(1)} fusion(bf16[640,15,128]{2,0,1:T(8,128)(2,1)} %get-tuple-element.219, s32[]{:T(128)S(6)} %select_n.164, bf16[640,15,128]{2,0,1:T(8,128)(2,1)} %get-tuple-element.218), kind=kOutput, calls=%fused_computation.17.clone.1 | convolution fusion | flops 524288000 | bytes 9831424 | tf_op jit(solution)/shard_map/while/body/eval_jaxpr/rhd,khd->hrk/dot_general | solution.py:45
  129.2 2.1 %fusion.49 = f32[5,640]{1,0:T(8,128)S(1)} fusion(f32[5,640,640]{1,2,0:T(8,128)S(1)} %fusion.48), kind=kOutput, calls=%fused_computation.73.clone.1 | output fusion | flops 8192639 | bytes 8204800 | tf_op jit(solution)/shard_map/while/body/eval_jaxpr/sub | solution.py:23
  132.4 8.7 %fusion.50 = bf16[640,5,128]{0,2,1:T(8,128)(2,1)S(1)} fusion(f32[5,640]{1,0:T(8,128)S(1)} %fusion.49, bf16[640,15,128]{2,0,1:T(8,128)(2,1)} %get-tuple-element.217, s32[]{:T(128)S(6)} %select_n.164, f32[5,640,640]{1,2,0:T(8,128)} %copy-done.3), kind=kOutput, calls=%fused_computation.16.clone.1 | convolution fusion | flops 534941440 | bytes 18035204 | tf_op jit(solution)/shard_map/while/body/eval_jaxpr/hrk,khd->rhd/dot_general | solution.py:49
  143.4 2.6 %fusion.48 = f32[5,640,640]{1,2,0:T(8,128)S(1)} fusion(bf16[640,15,128]{2,0,1:T(8,128)(2,1)} %get-tuple-element.219, s32[]{:T(128)S(6)} %select_n.164, bf16[640,15,128]{2,0,1:T(8,128)(2,1)} %get-tuple-element.218), kind=kOutput, calls=%fused_computation.17.clone.1 | convolution fusion | flops 524288000 | bytes 9831424 | tf_op jit(solution)/shard_map/while/body/eval_jaxpr/rhd,khd->hrk/dot_general | solution.py:45
  146.0 2.1 %fusion.49 = f32[5,640]{1,0:T(8,128)S(1)} fusion(f32[5,640,640]{1,2,0:T(8,128)S(1)} %fusion.48), kind=kOutput, calls=%fused_computation.73.clone.1 | output fusion | flops 8192639 | bytes 8204800 | tf_op jit(solution)/shard_map/while/body/eval_jaxpr/sub | solution.py:23
  149.2 8.7 %fusion.50 = bf16[640,5,128]{0,2,1:T(8,128)(2,1)S(1)} fusion(f32[5,640]{1,0:T(8,128)S(1)} %fusion.49, bf16[640,15,128]{2,0,1:T(8,128)(2,1)} %get-tuple-element.217, s32[]{:T(128)S(6)} %select_n.164, f32[5,640,640]{1,2,0:T(8,128)} %copy-done.3), kind=kOutput, calls=%fused_computation.16.clone.1 | convolution fusion | flops 534941440 | bytes 18035204 | tf_op jit(solution)/shard_map/while/body/eval_jaxpr/hrk,khd->rhd/dot_general | solution.py:49
  160.2 4.2 %exponential_reduce_fusion = (f32[2,20,10,8]{3,2,1,0:T(8,128)}, f32[2,20,10,8,8]{3,4,2,1,0:T(8,128)S(1)}) fusion(bf16[8,2,20,10,128]{4,3,2,1,0:T(8,128)(2,1)} %bitcast.13, bf16[8,2,20,10,128]{4,3,2,1,0:T(8,128)(2,1)} %bitcast.10, pred[10,8,8]{1,2,0:T(8,128)(4,1)S(1)} %broadcast_compare_fusion), kind=kOutput, calls=%fused_computation.43 | convolution fusion | flops 6656007 | bytes 1754240 | tf_op jit(solution)/shard_map/sub | solution.py:23
  164.4 1.8 fusion.24
  168.8 6.1 %all-to-all-start.3 = ((bf16[16,20,10,128]{3,1,2,0:T(8,128)(2,1)}), bf16[16,20,10,128]{3,1,2,0:T(8,128)(2,1)}, u32[]{:S(2)}, u32[]{:S(2)}) async-start(bf16[16,20,10,128]{3,1,2,0:T(8,128)(2,1)} %copy.104), calls=%async_computation.3 | async-start | bytes 1966080 | tf_op jit(solution)/shard_map/all_to_all | solution.py:89
  174.9 1.6 constant_dynamic-slice_fusion.1
  176.9 2.1 sort.32
  180.7 2.7 %maximum_select_fusion.3 = bf16[320,30,128]{2,0,1:T(8,128)(2,1)S(1)} fusion(bf16[320,15,128]{2,0,1:T(8,128)(2,1)} %copy-done.12, bf16[320,15,128]{2,0,1:T(8,128)(2,1)} %get-tuple-element.150, pred[]{:T(512)S(6)} %eq.4), kind=kLoop, calls=%fused_computation.36 | loop fusion | flops 3686400 | bytes 4915201 | tf_op jit(solution)/shard_map/jit(_where)/select_n | solution.py:140
  183.4 13.4 %all-to-all-done.3 = bf16[16,20,10,128]{3,1,2,0:T(8,128)(2,1)} async-done(((bf16[16,20,10,128]{3,1,2,0:T(8,128)(2,1)}), bf16[16,20,10,128]{3,1,2,0:T(8,128)(2,1)}, u32[]{:S(2)}, u32[]{:S(2)}) %all-to-all-start.3) | async-done | bytes 819232 | tf_op jit(solution)/shard_map/all_to_all | solution.py:89
  196.8 2.4 %copy.105 = bf16[16,20,10,128]{3,1,0,2:T(8,128)(2,1)} copy(bf16[16,20,10,128]{3,1,2,0:T(8,128)(2,1)} %all-to-all-done.3) | data formatting | bytes 1638400 | tf_op jit(solution)/shard_map/all_to_all | solution.py:89
  200.5 2.0 pad_maximum_fusion
  202.5 4.9 %gather_fusion.1 = bf16[40,320,128]{2,1,0:T(8,128)(2,1)} fusion(bf16[320,40,128]{2,0,1:T(8,128)(2,1)} %pad_maximum_fusion, s32[1024]{0:T(1024)S(1)} %pad_clamp_fusion), kind=kCustom, calls=%fused_computation.7 | custom fusion | bytes 6553760 | tf_op jit(solution)/shard_map/jit(_take)/gather | solution.py:145
  207.4 4.3 %bitcast_select_fusion = bf16[320,5120]{1,0:T(8,128)(2,1)} fusion(pred[5120]{0:T(1024)(128)(4,1)S(1)} %broadcast_bitcast_fusion, bf16[40,320,128]{2,1,0:T(8,128)(2,1)} %gather_fusion.1), kind=kLoop, calls=%fused_computation.28 | loop fusion | flops 1638400 | bytes 6558720 | tf_op jit(solution)/shard_map/jit(_take)/select_n | solution.py:145
  (64 shorter events, 19.4 us)
Async XLA Ops:
  0.0 1.9 copy-start
  0.0 4.5 %copy-start.13 = (s32[40]{0:T(128)S(1)}, s32[40]{0:T(128)}, u32[]{:S(2)}) copy-start(s32[40]{0:T(128)} %param.14) | copy-start | bytes 484
  6.7 4.7 %copy-start.4 = (bf16[320,40,128]{2,0,1:T(8,128)(2,1)S(1)}, bf16[320,40,128]{2,0,1:T(8,128)(2,1)}, u32[]{:S(2)}) copy-start(bf16[320,40,128]{2,0,1:T(8,128)(2,1)} %copy_bitcast_fusion.1) | copy-start | bytes 9830404
  29.4 34.9 %all-to-all-start.2 = ((bf16[1,320,10,128]{3,2,0,1:T(8,128)(2,1)}), bf16[1,320,10,128]{3,2,0,1:T(8,128)(2,1)}, u32[]{:S(2)}, u32[]{:S(2)}) async-start(bf16[1,320,10,128]{3,2,0,1:T(8,128)(2,1)} %copy.97), calls=%async_computation.2 | async-start | bytes 2621440 | tf_op jit(solution)/shard_map/all_to_all | solution.py:61
  43.5 4.4 %copy-start.5 = (bf16[30,320,128]{2,1,0:T(8,128)(2,1)S(1)}, bf16[30,320,128]{2,1,0:T(8,128)(2,1)}, u32[]{:S(2)}) copy-start(bf16[30,320,128]{2,1,0:T(8,128)(2,1)} %gather_fusion.4) | copy-start | bytes 7372804
  54.1 23.9 %collective-permute-start = (bf16[320,15,128]{2,0,1:T(8,128)(2,1)}, bf16[320,15,128]{2,0,1:T(8,128)(2,1)}, u32[]{:S(2)}, u32[]{:S(2)}) collective-permute-start(bf16[320,15,128]{2,0,1:T(8,128)(2,1)} %get-tuple-element.157), channel_id=1, source_target_pairs={{0,1},{1,0},{2,3},{3,2},{4,5},{5,4},{6,7},{7,6},{8,9},{9,8},{10,11... | collective-permute-start | bytes 3686408 | tf_op jit(solution)/shard_map/ppermute | solution.py:18
  54.5 1.8 copy-start.11
  56.1 16.3 %copy-start.6 = (bf16[320,30,128]{2,0,1:T(8,128)(2,1)S(1)}, bf16[320,30,128]{2,0,1:T(8,128)(2,1)}, u32[]{:S(2)}) copy-start(bf16[320,30,128]{2,0,1:T(8,128)(2,1)} %get-tuple-element.158) | copy-start | bytes 7372804
  56.1 26.0 %collective-permute-start.1 = (bf16[320,15,128]{2,0,1:T(8,128)(2,1)}, bf16[320,15,128]{2,0,1:T(8,128)(2,1)}, u32[]{:S(2)}, u32[]{:S(2)}) collective-permute-start(bf16[320,15,128]{2,0,1:T(8,128)(2,1)} %get-tuple-element.155), channel_id=1, source_target_pairs={{0,1},{1,0},{2,3},{3,2},{4,5},{5,4},{6,7},{7,6},{8,9},{9,8},{10,11... | collective-permute-start | bytes 3686408 | tf_op jit(solution)/shard_map/ppermute | solution.py:18
  64.3 35.5 %all-to-all-start.1 = ((bf16[1,320,10,128]{3,2,0,1:T(8,128)(2,1)}), bf16[1,320,10,128]{3,2,0,1:T(8,128)(2,1)}, u32[]{:S(2)}, u32[]{:S(2)}) async-start(bf16[1,320,10,128]{3,2,0,1:T(8,128)(2,1)} %copy.94), calls=%async_computation.1 | async-start | bytes 2621440 | tf_op jit(solution)/shard_map/all_to_all | solution.py:60
  72.4 4.8 %copy-start.2 = (s32[40]{0:T(128)S(1)}, s32[40]{0:T(128)}, u32[]{:S(2)}) copy-start(s32[40]{0:T(128)} %param.15) | copy-start | bytes 484
  74.1 4.0 %copy-start.8 = (bf16[320,15,128]{2,0,1:T(8,128)(2,1)S(1)}, bf16[320,15,128]{2,0,1:T(8,128)(2,1)}, u32[]{:S(2)}) copy-start(bf16[320,15,128]{2,0,1:T(8,128)(2,1)} %get-tuple-element.156) | copy-start | bytes 3686404
  74.1 11.9 %collective-permute-start.2 = (bf16[320,15,128]{2,0,1:T(8,128)(2,1)}, bf16[320,15,128]{2,0,1:T(8,128)(2,1)}, u32[]{:S(2)}, u32[]{:S(2)}) collective-permute-start(bf16[320,15,128]{2,0,1:T(8,128)(2,1)} %get-tuple-element.153), channel_id=1, source_target_pairs={{0,1},{1,0},{2,3},{3,2},{4,5},{5,4},{6,7},{7,6},{8,9},{9,8},{10,11... | collective-permute-start | bytes 3686408 | tf_op jit(solution)/shard_map/ppermute | solution.py:18
  78.0 4.0 %copy-start.9 = (bf16[320,15,128]{2,0,1:T(8,128)(2,1)S(1)}, bf16[320,15,128]{2,0,1:T(8,128)(2,1)}, u32[]{:S(2)}) copy-start(bf16[320,15,128]{2,0,1:T(8,128)(2,1)} %get-tuple-element.154) | copy-start | bytes 3686404
  82.0 4.0 %copy-start.10 = (bf16[320,15,128]{2,0,1:T(8,128)(2,1)S(1)}, bf16[320,15,128]{2,0,1:T(8,128)(2,1)}, u32[]{:S(2)}) copy-start(bf16[320,15,128]{2,0,1:T(8,128)(2,1)} %get-tuple-element.152) | copy-start | bytes 3686404
  99.9 64.5 %all-to-all-start = ((bf16[1,320,10,128]{3,2,0,1:T(8,128)(2,1)}), bf16[1,320,10,128]{3,2,0,1:T(8,128)(2,1)S(1)}, u32[]{:S(2)}, u32[]{:S(2)}) async-start(bf16[1,320,10,128]{3,2,0,1:T(8,128)(2,1)} %copy.91), calls=%async_computation | async-start | bytes 2621440 | tf_op jit(solution)/shard_map/all_to_all | solution.py:62
  112.4 3.2 %copy-start.3 = (f32[5,640,640]{1,2,0:T(8,128)}, f32[5,640,640]{1,2,0:T(8,128)S(1)}, u32[]{:S(2)}) copy-start(f32[5,640,640]{1,2,0:T(8,128)S(1)} %fusion.48) | copy-start | bytes 24576004 | tf_op jit(solution)/shard_map/while
  129.2 3.2 %copy-start.3 = (f32[5,640,640]{1,2,0:T(8,128)}, f32[5,640,640]{1,2,0:T(8,128)S(1)}, u32[]{:S(2)}) copy-start(f32[5,640,640]{1,2,0:T(8,128)S(1)} %fusion.48) | copy-start | bytes 24576004 | tf_op jit(solution)/shard_map/while
  146.0 3.2 %copy-start.3 = (f32[5,640,640]{1,2,0:T(8,128)}, f32[5,640,640]{1,2,0:T(8,128)S(1)}, u32[]{:S(2)}) copy-start(f32[5,640,640]{1,2,0:T(8,128)S(1)} %fusion.48) | copy-start | bytes 24576004 | tf_op jit(solution)/shard_map/while
  166.2 8.7 %copy-start.7 = (bf16[640,15,128]{2,0,1:T(8,128)(2,1)S(1)}, bf16[640,15,128]{2,0,1:T(8,128)(2,1)}, u32[]{:S(2)}) copy-start(bf16[640,15,128]{2,0,1:T(8,128)(2,1)} %get-tuple-element.105) | copy-start | bytes 7372804
  168.8 28.0 %all-to-all-start.3 = ((bf16[16,20,10,128]{3,1,2,0:T(8,128)(2,1)}), bf16[16,20,10,128]{3,1,2,0:T(8,128)(2,1)}, u32[]{:S(2)}, u32[]{:S(2)}) async-start(bf16[16,20,10,128]{3,1,2,0:T(8,128)(2,1)} %copy.104), calls=%async_computation.3 | async-start | bytes 1966080 | tf_op jit(solution)/shard_map/all_to_all | solution.py:89
  176.5 3.1 %collective-permute-start.3 = (bf16[320,15,128]{2,0,1:T(8,128)(2,1)}, bf16[320,15,128]{2,0,1:T(8,128)(2,1)S(1)}, u32[]{:S(2)}, u32[]{:S(2)}) collective-permute-start(bf16[320,15,128]{2,0,1:T(8,128)(2,1)} %get-tuple-element.151), channel_id=1, source_target_pairs={{0,1},{1,0},{2,3},{3,2},{4,5},{5,4},{6,7},{7,6},{8,9},{9,8},{10,11... | collective-permute-start | bytes 3686408 | tf_op jit(solution)/shard_map/ppermute | solution.py:18
  179.7 1.0 copy-start.12
  202.5 9.2 %copy-start.1 = (bf16[320,5120]{1,0:T(8,128)(2,1)S(1)}, bf16[320,5120]{1,0:T(8,128)(2,1)}, u32[]{:S(2)}) copy-start(bf16[320,5120]{1,0:T(8,128)(2,1)} %param.11) | copy-start | bytes 9830404
where the time goes:
time: 213 us; the launch traced here: 212 us
  local copies, waits for them, and re-layouts  71.1 us (33%)
  matrix products  39.9 us (19%)
  other arithmetic  39.1 us (18%)
  starting transfers between devices  30.8 us (14%)
  waiting for transfers between devices  30.5 us (14%)
    dot_general x3, matrix products, one_block(): jnp.einsum('hrk,khd->rhd', weights, value_block, preferred_element_type=j...  26 us
    all_to_all x1, waiting for transfers between devices, attend_columns(): lax.all_to_all(output, 'frame', split_axis=0, concat_axis=1, tiled=True)  13.4 us
    select_n x3, other arithmetic, whole_frame(): jnp.where(parity == 0, jnp.concatenate([own, got], axis=0), jnp.concatena...  11.7 us
    all_to_all x1, waiting for transfers between devices, attend_columns(): lax.all_to_all(query_part[None], 'frame', split_axis=1, concat_axis=0, ti...  10.1 us
    all_to_all x1, starting transfers between devices, attend_columns(): lax.all_to_all(query_part[None], 'frame', split_axis=1, concat_axis=0, ti...  8.06 us
    all_to_all x1, starting transfers between devices, attend_columns(): lax.all_to_all(value_part[None], 'frame', split_axis=1, concat_axis=0, ti...  8.02 us
    dot_general x3, matrix products, one_block(): jnp.einsum('rhd,khd->hrk', query_block, key_block, preferred_element_type...  7.84 us
    all_to_all x1, starting transfers between devices, attend_columns(): lax.all_to_all(key_part[None], 'frame', split_axis=1, concat_axis=0, tile...  7.43 us
  transfers between devices with their start and end apart: 8, of which 4 were waited for; matrix products, arithmetic and copies ran while one was open for 46% of the time, Pallas kernels for 0%

commit v1 on v0

v1 whole, which is shorter than its diff:
```python
import functools
import math

import jax
import jax.numpy as jnp
from jax import lax
from jax.experimental import pallas as pl
from jax.experimental.pallas import tpu as pltpu
from jax.sharding import PartitionSpec as P

TEMP_HEADS = 10
HEAD_DIM = 128
PIXEL_BLOCK = 32
SPATIAL_PIECES = 3
MASKED = -1e30
VMEM_BYTES = 48 * 1024 * 1024


def swap_bit(block, bit):
    count = lax.axis_size("frame")
    return lax.ppermute(block, "frame", [(i, i ^ (1 << bit)) for i in range(count)])


def shift_pairs(block, step):
    count = lax.axis_size("frame")
    route = [(i, i + 4 * step) for i in range(count) if 0 <= i + 4 * step < count]
    return lax.ppermute(block, "frame", route)


def extract_kernel(
    place, labels, band, queries, keys, values,
    meta, pair_keep, pair_send, query_keep, query_send, sems,
):
    heads = labels.shape[0]
    half = query_keep.shape[1]
    side = place[0]

    def one_head(head, counts):
        spatial, temporal = counts
        is_temporal = labels[head] == 1

        @pl.when(is_temporal)
        def _():
            meta[heads + temporal] = head
            meta[2 * heads + temporal] = band[head]
            columns = pl.ds(pl.multiple_of(head * HEAD_DIM, HEAD_DIM), HEAD_DIM)
            kept = pl.ds(pl.multiple_of(side * half, half), half)
            sent = pl.ds(pl.multiple_of((1 - side) * half, half), half)
            for number, source in enumerate((keys, values)):
                pltpu.make_async_copy(source.at[kept, columns], pair_keep.at[number, temporal], sems.at[0]).start()
                pltpu.make_async_copy(source.at[sent, columns], pair_send.at[number, temporal], sems.at[1]).start()
            pltpu.make_async_copy(queries.at[kept, columns], query_keep.at[temporal], sems.at[2]).start()
            pltpu.make_async_copy(queries.at[sent, columns], query_send.at[temporal], sems.at[3]).start()

        @pl.when(jnp.logical_not(is_temporal))
        def _():
            meta[spatial] = head

        step = is_temporal.astype(jnp.int32)
        return spatial + 1 - step, temporal + step

    lax.fori_loop(0, heads, one_head, (jnp.int32(0), jnp.int32(0)))
    for number, whole in enumerate((pair_keep, pair_send, query_keep, query_send)):
        pltpu.make_async_copy(whole, whole, sems.at[number]).wait()


def extract(place, labels, band, queries, keys, values):
    rows = queries.shape[0]
    half = rows // 2
    pair = jax.ShapeDtypeStruct((2, TEMP_HEADS, half, HEAD_DIM), jnp.bfloat16)
    single = jax.ShapeDtypeStruct((TEMP_HEADS, half, HEAD_DIM), jnp.bfloat16)
    any_spec = pl.BlockSpec(memory_space=pl.ANY)
    smem_spec = pl.BlockSpec(memory_space=pltpu.SMEM)
    return pl.pallas_call(
        extract_kernel,
        out_shape=(jax.ShapeDtypeStruct((3 * labels.shape[0],), jnp.int32), pair, pair, single, single),
        in_specs=[smem_spec] * 3 + [any_spec] * 3,
        out_specs=(smem_spec,) + (any_spec,) * 4,
        scratch_shapes=[pltpu.SemaphoreType.DMA((4,))],
        cost_estimate=pl.CostEstimate(flops=0, bytes_accessed=12 * TEMP_HEADS * half * HEAD_DIM * 2, transcendentals=0),
        name="extract_temporal",
    )(place, labels, band, queries, keys, values)


def spatial_kernel(scale, meta, query, key_own, value_own, key_far, value_far, *rest):
    out, key_all, value_all = rest[-3:]
    rows = query.shape[0]
    key_all[:rows, :] = key_own[...]
    key_all[rows:, :] = key_far[...]
    value_all[:rows, :HEAD_DIM] = value_own[...]
    value_all[rows:, :HEAD_DIM] = value_far[...]
    value_all[:, HEAD_DIM:] = jnp.ones((2 * rows, HEAD_DIM), jnp.bfloat16)
    chunk = 64
    for start in range(0, rows, chunk):
        scores = lax.dot_general(
            query[start : start + chunk, :], key_all[...], (((1,), (1,)), ((), ())), preferred_element_type=jnp.float32
        )
        peak = jnp.max(scores, axis=1, keepdims=True)
        weights = jnp.exp2((scores - peak) * scale).astype(jnp.bfloat16)
        both = jnp.dot(weights, value_all[...], preferred_element_type=jnp.float32)
        out[start : start + chunk, :] = (both[:, :HEAD_DIM] / both[:, HEAD_DIM:]).astype(jnp.bfloat16)


def spatial_piece(meta, first, count, queries, keys, values, keys_far, values_far, so_far):
    rows = queries.shape[0]
    block = pl.BlockSpec((rows, HEAD_DIM), lambda i, meta: (0, meta[first + i]))
    operands = [queries, keys, values, keys_far, values_far]
    specs = [block] * 5
    aliases = {}
    if so_far is not None:
        operands.append(so_far)
        specs.append(pl.BlockSpec(memory_space=pl.ANY))
        aliases = {6: 0}
    return pl.pallas_call(
        functools.partial(spatial_kernel, math.log2(math.e) / math.sqrt(HEAD_DIM)),
        out_shape=jax.ShapeDtypeStruct(queries.shape, jnp.bfloat16),
        grid_spec=pltpu.PrefetchScalarGridSpec(
            num_scalar_prefetch=1,
            grid=(count,),
            in_specs=specs,
            out_specs=block,
            scratch_shapes=[
                pltpu.VMEM((2 * rows, HEAD_DIM), jnp.bfloat16),
                pltpu.VMEM((2 * rows, 2 * HEAD_DIM), jnp.bfloat16),
            ],
        ),
        input_output_aliases=aliases,
        compiler_params=pltpu.CompilerParams(vmem_limit_bytes=VMEM_BYTES),
        cost_estimate=pl.CostEstimate(
            flops=count * rows * 2 * rows * HEAD_DIM * 2 * 3,
            bytes_accessed=count * 6 * rows * HEAD_DIM * 2,
            transcendentals=count * rows * 2 * rows,
        ),
        name="spatial_heads",
    )(meta, *operands)


def temporal_kernel(scale, shifts, meta, place, query_own, query_far, *rest):
    pairs, (out_own, out_far) = rest[:-2], rest[-2:]
    slots = len(pairs)
    half = query_own.shape[1]
    heads = meta.shape[0] // 3
    band = meta[2 * heads + pl.program_id(0)]
    side, pair_number, frames = place[0], place[1], place[2]
    size = PIXEL_BLOCK
    row = lax.broadcasted_iota(jnp.int32, (2 * size, slots * size), 0)
    column = lax.broadcasted_iota(jnp.int32, (2 * size, slots * size), 1)
    row_frame = 2 * pair_number + jnp.where(row >= size, 1 - side, side)
    slot = column // size
    column_frame = 2 * pair_number + jnp.where(slot % 2 == 1, 1 - side, side)
    shift = jnp.zeros_like(slot)
    for number, step in enumerate(shifts):
        shift = jnp.where(slot // 2 == number, step, shift)
    column_frame = column_frame + 2 * shift
    keep = (
        (row % size == column % size)
        & (jnp.abs(row_frame - column_frame) <= band)
        & (column_frame >= 0)
        & (column_frame < frames)
    )
    for start in range(0, half, size):
        part = slice(start, start + size)
        query = jnp.concatenate([query_own[0, part, :], query_far[0, part, :]], axis=0)
        key = jnp.concatenate([pair[0, 0, part, :] for pair in pairs], axis=0)
        value = jnp.concatenate([pair[1, 0, part, :] for pair in pairs], axis=0)
        scores = lax.dot_general(query, key, (((1,), (1,)), ((), ())), preferred_element_type=jnp.float32)
        scores = jnp.where(keep, scores, MASKED)
        peak = jnp.max(scores, axis=1, keepdims=True)
        weights = jnp.where(keep, jnp.exp2((scores - peak) * scale), 0.0)
        total = jnp.sum(weights, axis=1, keepdims=True)
        result = jnp.dot(weights.astype(jnp.bfloat16), value, preferred_element_type=jnp.float32) / total
        out_own[0, part, :] = result[:size].astype(jnp.bfloat16)
        out_far[0, part, :] = result[size:].astype(jnp.bfloat16)


def temporal(meta, place, shifts, query_own, query_far, pairs):
    half = query_own.shape[1]
    single = pl.BlockSpec((1, half, HEAD_DIM), lambda i, *_: (i, 0, 0))
    double = pl.BlockSpec((2, 1, half, HEAD_DIM), lambda i, *_: (0, i, 0, 0))
    out = jax.ShapeDtypeStruct(query_own.shape, jnp.bfloat16)
    return pl.pallas_call(
        functools.partial(temporal_kernel, math.log2(math.e) / math.sqrt(HEAD_DIM), shifts),
        out_shape=(out, out),
        grid_spec=pltpu.PrefetchScalarGridSpec(
            num_scalar_prefetch=2,
            grid=(TEMP_HEADS,),
            in_specs=[single, single] + [double] * len(pairs),
            out_specs=(single, single),
        ),
        compiler_params=pltpu.CompilerParams(vmem_limit_bytes=VMEM_BYTES),
        cost_estimate=pl.CostEstimate(
            flops=TEMP_HEADS * half * len(pairs) * PIXEL_BLOCK * HEAD_DIM * 8,
            bytes_accessed=TEMP_HEADS * half * HEAD_DIM * 2 * (4 + 2 * len(pairs)),
            transcendentals=TEMP_HEADS * half * 2 * len(pairs) * PIXEL_BLOCK,
        ),
        name="temporal_heads",
    )(meta, place, query_own, query_far, *pairs)


def finish_kernel(meta, place, own, far, so_far, out, sems):
    heads = meta.shape[0] // 3
    half = own.shape[1]
    side = place[0]
    for number in range(TEMP_HEADS):
        columns = pl.ds(pl.multiple_of(meta[heads + number] * HEAD_DIM, HEAD_DIM), HEAD_DIM)
        for rows_of, source, sem in ((side, own, 0), (1 - side, far, 1)):
            rows = pl.ds(pl.multiple_of(rows_of * half, half), half)
            pltpu.make_async_copy(source.at[number], out.at[rows, columns], sems.at[sem]).start()
    for sem, whole in enumerate((own, far)):
        pltpu.make_async_copy(whole, whole, sems.at[sem]).wait()


def finish(meta, place, own, far, so_far):
    any_spec = pl.BlockSpec(memory_space=pl.ANY)
    smem_spec = pl.BlockSpec(memory_space=pltpu.SMEM)
    return pl.pallas_call(
        finish_kernel,
        out_shape=jax.ShapeDtypeStruct(so_far.shape, so_far.dtype),
        in_specs=[smem_spec] * 2 + [any_spec] * 3,
        out_specs=any_spec,
        scratch_shapes=[pltpu.SemaphoreType.DMA((2,))],
        input_output_aliases={4: 0},
        cost_estimate=pl.CostEstimate(flops=0, bytes_accessed=4 * own.size * 2, transcendentals=0),
        name="finish",
    )(meta, place, own, far, so_far)


def shards(queries, keys, values, labels, band):
    count = lax.axis_size("frame")
    frames = count // 2
    index = lax.axis_index("frame").astype(jnp.int32)
    place = jnp.stack([(index // 2) % 2, index // 4, jnp.int32(frames)])
    reach = frames // 4

    keys_far = swap_bit(keys, 0)
    values_far = swap_bit(values, 0)
    meta, pair_keep, pair_send, query_keep, query_send = extract(place, labels, band, queries, keys, values)
    pair_got = swap_bit(pair_send, 1)
    query_got = swap_bit(query_send, 1)

    shifts, pairs = [0], [pair_keep, pair_got]
    below, above = [pair_keep, pair_got], [pair_keep, pair_got]
    for step in range(1, reach + 1):
        below = [shift_pairs(block, 1) for block in below]
        above = [shift_pairs(block, -1) for block in above]
        shifts += [-step, step]
        pairs += below + above

    heads = labels.shape[0]
    spatial_count = heads - TEMP_HEADS
    piece = spatial_count // SPATIAL_PIECES
    result = None
    for number in range(SPATIAL_PIECES):
        result = spatial_piece(meta, number * piece, piece, queries, keys, values, keys_far, values_far, result)

    out_keep, out_send = temporal(meta, place, tuple(shifts), query_keep, query_got, pairs)
    out_got = swap_bit(out_send, 1)
    return finish(meta, place, out_keep, out_got, result)


def solution(mesh):
    placed = (
        P(("group", "frame"), None),
        P(("group", "frame"), None),
        P(("group", "frame"), None),
        P("group"),
        P("group"),
    )
    return jax.shard_map(
        shards, mesh=mesh, in_specs=placed, out_specs=P(("group", "frame"), None), check_vma=False
    )
```

time: 213 us -> 279 us (1.31)
  Pallas kernels: 0 us -> 181 us
  local copies, waits for them, and re-layouts: 71.1 us -> 6.15 us
  matrix products: 39.9 us -> 0 us
  other arithmetic: 39.1 us -> 0.56 us
  waiting for transfers between devices: 30.5 us -> 64.2 us
  starting transfers between devices: 30.8 us -> 26.5 us
    pallas_call x0 -> x6, Pallas kernels: none -> 181 us  [the longest x1 76.9 us: extract(): pl.pallas_call(extract_kernel, out_shape=(jax.ShapeDtypeStruct((3 * label...]
    ppermute x4 -> x13, waiting for transfers between devices: 0.62 us -> 64.2 us  [the longest x8 42.3 us: shift_pairs(): return lax.ppermute(block, 'frame', route)]
    dot_general x7 -> x0, matrix products: 35.7 us -> none  [the longest x3 26 us: one_block(): jnp.einsum('hrk,khd->rhd', weights, value_block, preferred_element_type=j...]
    all_to_all x4 -> x0, waiting for transfers between devices: 29.9 us -> none  [the longest x1 13.4 us: attend_columns(): lax.all_to_all(output, 'frame', split_axis=0, concat_axis=1, tiled=True)]
    all_to_all x4 -> x0, starting transfers between devices: 29.6 us -> none  [the longest x1 8.06 us: attend_columns(): lax.all_to_all(query_part[None], 'frame', split_axis=1, concat_axis=0, ti...]
    ppermute x4 -> x13, starting transfers between devices: 1.23 us -> 26.5 us  [the longest x8 21.3 us: shift_pairs(): return lax.ppermute(block, 'frame', route)]
    gather x8 -> x0, local copies, waits for them, and re-layouts: 25.3 us -> none  [the longest x1 4.91 us: shards(): jnp.take(jnp.concatenate([spatial, temporal], axis=1), inverse, axis=1)]
    select_n x8 -> x0, other arithmetic: 23.4 us -> none  [the longest x3 11.7 us: whole_frame(): jnp.where(parity == 0, jnp.concatenate([own, got], axis=0), jnp.concatena...]
  transfers between devices with their start and end apart: 8 -> 13, of which waited for: 4 -> 6; matrix products, arithmetic and copies ran while one was open for 46% -> 0% of each run, Pallas kernels for 0% -> 55%
where the time goes in v1:
time: 279 us; the launch traced here: 278 us
  Pallas kernels  181 us (65%)
  waiting for transfers between devices  64.2 us (23%)
  starting transfers between devices  26.5 us (9%)
  local copies, waits for them, and re-layouts  6.15 us (2%)
    pallas_call x1, Pallas kernels, extract(): pl.pallas_call(extract_kernel, out_shape=(jax.ShapeDtypeStruct((3 * label...  76.9 us
    pallas_call x3, Pallas kernels, spatial_piece(): pl.pallas_call(functools.partial(spatial_kernel, math.log2(math.e) / math...  60.8 us
    ppermute x8, waiting for transfers between devices, shift_pairs(): return lax.ppermute(block, 'frame', route)  42.3 us
    pallas_call x1, Pallas kernels, finish(): pl.pallas_call(finish_kernel, out_shape=jax.ShapeDtypeStruct(so_far.shape...  26.6 us
    ppermute x5, waiting for transfers between devices, swap_bit(): lax.ppermute(block, 'frame', [(i, i ^ 1 << bit) for i in range(count)])  22 us
    ppermute x8, starting transfers between devices, shift_pairs(): return lax.ppermute(block, 'frame', route)  21.3 us
    pallas_call x1, Pallas kernels, temporal(): pl.pallas_call(functools.partial(temporal_kernel, math.log2(math.e) / mat...  16.4 us
    unnamed x26, local copies, waits for them, and re-layouts  6.15 us
  transfers between devices with their start and end apart: 13, of which 6 were waited for; matrix products, arithmetic and copies ran while one was open for 0% of the time, Pallas kernels for 55%

profile of v1, /device:TPU:0, one launch (start us, length us, event | category | flops | bytes accessed | tf_op | source)
XLA Modules:
  0.0 278.3 jit_solution(5150345860217358134)
XLA Ops:
  0.0 0.5 collective-permute-start.11
  0.5 0.1 collective-permute-start.12
  0.5 0.6 pad_add_fusion.place
  1.1 76.9 %extract_temporal.1 = (s32[120]{0:T(128)}, bf16[2,10,160,128]{3,2,1,0:T(8,128)(2,1)}, bf16[2,10,160,128]{3,2,1,0:T(8,128)(2,1)}, bf16[10,160,128]{2,1,0:T(8,128)(2,1)}, bf16[10,160,128]{2,1,0:T(8,128)(2,1)}) custom-call(s32[3]{0:T(128)} %pad_add_fusion.place, s32[40]{0:T(128)} %labels.1, s32[40]{0:T(128)} %band.1, bf16[320,5120]{1,0:T(8,128)(2,1)} %query.5, ...), custom_call_target="tpu_custom_call" | custom-call | bytes 4915200 | tf_op jit(solution)/shard_map/extract_temporal/pallas_call | solution.py:74
  78.0 3.0 %collective-permute-start = (bf16[10,160,128]{2,1,0:T(8,128)(2,1)}, bf16[10,160,128]{2,1,0:T(8,128)(2,1)S(1)}, u32[]{:S(2)}, u32[]{:S(2)}) collective-permute-start(bf16[10,160,128]{2,1,0:T(8,128)(2,1)} %get-tuple-element.14), channel_id=1, source_target_pairs={{0,2},{1,3},{2,0},{3,1},{4,6},{5,7},{6,4},{7,5},{8,10},{9,11},{10,... | collective-permute-start | bytes 1228808 | tf_op jit(solution)/shard_map/ppermute | solution.py:21
  81.0 0.1 collective-permute-start.1
  81.1 1.3 collective-permute-start.4
  82.4 9.1 %collective-permute-done.query_far = bf16[10,160,128]{2,1,0:T(8,128)(2,1)S(1)} collective-permute-done((bf16[10,160,128]{2,1,0:T(8,128)(2,1)}, bf16[10,160,128]{2,1,0:T(8,128)(2,1)S(1)}, u32[]{:S(2)}, u32[]{:S(2)}) %collective-permute-start) | collective-permute-done | bytes 409632 | tf_op jit(solution)/shard_map/ppermute | solution.py:21
  91.5 4.1 %collective-permute-start.2 = (bf16[2,10,160,128]{3,2,1,0:T(8,128)(2,1)}, bf16[2,10,160,128]{3,2,1,0:T(8,128)(2,1)S(1)}, u32[]{:S(2)}, u32[]{:S(2)}) collective-permute-start(bf16[2,10,160,128]{3,2,1,0:T(8,128)(2,1)} %get-tuple-element.15.rest_0_), channel_id=1, source_target_pairs={{0,4},{1,5},{2,6},{3,7},{4,8},{5,9},{6,10},{7,11},{8,12},{9,13},{1... | collective-permute-start | bytes 2457608 | tf_op jit(solution)/shard_map/ppermute | solution.py:27
  95.6 12.8 %collective-permute-done.1.rest_1_ = bf16[2,10,160,128]{3,2,1,0:T(8,128)(2,1)S(1)} collective-permute-done((bf16[2,10,160,128]{3,2,1,0:T(8,128)(2,1)}, bf16[2,10,160,128]{3,2,1,0:T(8,128)(2,1)S(1)}, u32[]{:S(2)}, u32[]{:S(2)}) %collective-permute-start.1) | collective-permute-done | bytes 819232 | tf_op jit(solution)/shard_map/ppermute | solution.py:21
  108.4 1.3 collective-permute-start.5
  109.7 0.0 collective-permute-done.4.rest_4_
  109.7 4.6 %collective-permute-start.3 = (bf16[2,10,160,128]{3,2,1,0:T(8,128)(2,1)S(1)}, bf16[2,10,160,128]{3,2,1,0:T(8,128)(2,1)S(1)}, u32[]{:S(2)}, u32[]{:S(2)}) collective-permute-start(bf16[2,10,160,128]{3,2,1,0:T(8,128)(2,1)S(1)} %collective-permute-done.1.rest_1_), channel_id=1, source_target_pairs={{0,4},{1,5},{2,6},{3,7},{4,8},{5,9},{6,10},{7,11},{8,12},{9,13},{1... | collective-permute-start | bytes 2457608 | tf_op jit(solution)/shard_map/ppermute | solution.py:27
  114.3 0.0 collective-permute-done.2.rest_2_
  114.3 1.3 collective-permute-start.8
  115.7 15.8 %collective-permute-done.5.rest_5_ = bf16[2,10,160,128]{3,2,1,0:T(8,128)(2,1)S(1)} collective-permute-done((bf16[2,10,160,128]{3,2,1,0:T(8,128)(2,1)S(1)}, bf16[2,10,160,128]{3,2,1,0:T(8,128)(2,1)S(1)}, u32[]{:S(2)}, u32[]{:S(2)}) %collective-permute-start.5) | collective-permute-done | bytes 819232 | tf_op jit(solution)/shard_map/ppermute | solution.py:27
  131.5 3.7 %collective-permute-start.6 = (bf16[2,10,160,128]{3,2,1,0:T(8,128)(2,1)S(1)}, bf16[2,10,160,128]{3,2,1,0:T(8,128)(2,1)S(1)}, u32[]{:S(2)}, u32[]{:S(2)}) collective-permute-start(bf16[2,10,160,128]{3,2,1,0:T(8,128)(2,1)S(1)} %collective-permute-done.2.rest_2_), channel_id=1, source_target_pairs={{0,4},{1,5},{2,6},{3,7},{4,8},{5,9},{6,10},{7,11},{8,12},{9,13},{1... | collective-permute-start | bytes 2457608 | tf_op jit(solution)/shard_map/ppermute | solution.py:27
  135.2 0.0 collective-permute-done.3.rest_3_
  135.3 1.3 collective-permute-start.9
  136.6 12.5 %collective-permute-done.8.rest_8_ = bf16[2,10,160,128]{3,2,1,0:T(8,128)(2,1)S(1)} collective-permute-done((bf16[2,10,160,128]{3,2,1,0:T(8,128)(2,1)S(1)}, bf16[2,10,160,128]{3,2,1,0:T(8,128)(2,1)S(1)}, u32[]{:S(2)}, u32[]{:S(2)}) %collective-permute-start.8) | collective-permute-done | bytes 819232 | tf_op jit(solution)/shard_map/ppermute | solution.py:27
  149.1 3.7 %collective-permute-start.7 = (bf16[2,10,160,128]{3,2,1,0:T(8,128)(2,1)S(1)}, bf16[2,10,160,128]{3,2,1,0:T(8,128)(2,1)S(1)}, u32[]{:S(2)}, u32[]{:S(2)}) collective-permute-start(bf16[2,10,160,128]{3,2,1,0:T(8,128)(2,1)S(1)} %collective-permute-done.3.rest_3_), channel_id=1, source_target_pairs={{0,4},{1,5},{2,6},{3,7},{4,8},{5,9},{6,10},{7,11},{8,12},{9,13},{1... | collective-permute-start | bytes 2457608 | tf_op jit(solution)/shard_map/ppermute | solution.py:27
  152.8 0.0 collective-permute-done.6.rest_6_
  152.8 0.0 copy-start.9
  152.8 12.2 %collective-permute-done.9.rest_9_ = bf16[2,10,160,128]{3,2,1,0:T(8,128)(2,1)S(1)} collective-permute-done((bf16[2,10,160,128]{3,2,1,0:T(8,128)(2,1)S(1)}, bf16[2,10,160,128]{3,2,1,0:T(8,128)(2,1)S(1)}, u32[]{:S(2)}, u32[]{:S(2)}) %collective-permute-start.9) | collective-permute-done | bytes 819232 | tf_op jit(solution)/shard_map/ppermute | solution.py:27
  165.0 1.7 collective-permute-done.7.rest_7_
  166.8 0.0 copy-done.7
  166.8 0.0 copy-done.8
  166.8 0.0 copy-done.9
  166.8 0.0 copy-done.10
  166.8 0.9 copy-done.11
  167.7 0.0 copy-done.5
  167.7 1.1 copy-done.1
  168.8 1.0 copy-done.2
  169.8 0.6 copy-done.4
  170.4 16.4 %temporal_heads.1 = (bf16[10,160,128]{2,1,0:T(8,128)(2,1)S(1)}, bf16[10,160,128]{2,1,0:T(8,128)(2,1)S(1)}) custom-call(s32[120]{0:T(128)S(1)} %copy-done.4, s32[3]{0:T(128)S(1)} %copy-done.5, bf16[10,160,128]{2,1,0:T(8,128)(2,1)S(1)} %copy-done.2, bf16[10,160,128]{2,1,0:T(8,128)(2,1)S(1)} %collective-permute-done.query_far, ...), custom_call_target="tpu_custom_call" | custom-call | flops 524288000 | bytes 9830400 | tf_op jit(solution)/shard_map/temporal_heads/pallas_call | solution.py:181
  186.8 0.0 copy-start.3
  186.9 1.6 collective-permute-start.10
  188.4 0.0 collective-permute-done.11.key_far
  188.4 0.0 collective-permute-done.12.value_far
  188.5 1.7 copy-done.6
  190.2 0.0 copy-done
  190.2 20.3 %spatial_heads.3.rest_0_ = bf16[320,5120]{1,0:T(8,128)(2,1)} custom-call(s32[120]{0:T(128)S(1)} %copy-done.4, bf16[320,5120]{1,0:T(8,128)(2,1)S(1)} %copy-done, bf16[320,5120]{1,0:T(8,128)(2,1)} %key_own.5, bf16[320,5120]{1,0:T(8,128)(2,1)} %value_own.5, bf16[320,5120]{1,0:T(8,128)(2,1)} %copy-done.6, bf16[320,5120]{1,0:T(8,128)(2,1)} %collective-permute-done.12.value_far), custom_call_target="tpu_custom_call" | custom-call | flops 1572864000 | bytes 4915200 | tf_op jit(solution)/shard_map/spatial_heads/pallas_call | solution.py:114
  210.4 0.0 copy-done.3
  210.4 20.3 %spatial_heads.4.rest_0_ = bf16[320,5120]{1,0:T(8,128)(2,1)} custom-call(s32[120]{0:T(128)S(1)} %copy-done.4, bf16[320,5120]{1,0:T(8,128)(2,1)S(1)} %copy-done, bf16[320,5120]{1,0:T(8,128)(2,1)} %key_own.5, bf16[320,5120]{1,0:T(8,128)(2,1)} %value_own.5, bf16[320,5120]{1,0:T(8,128)(2,1)} %copy-done.6, ...), custom_call_target="tpu_custom_call", output_to_operand_aliasing={{}: (6, {})} | custom-call | flops 1572864000 | bytes 4915200 | tf_op jit(solution)/shard_map/spatial_heads/pallas_call | solution.py:114
  230.7 20.3 %spatial_heads.5.so_far = bf16[320,5120]{1,0:T(8,128)(2,1)} custom-call(s32[120]{0:T(128)S(1)} %copy-done.4, bf16[320,5120]{1,0:T(8,128)(2,1)S(1)} %copy-done, bf16[320,5120]{1,0:T(8,128)(2,1)} %key_own.5, bf16[320,5120]{1,0:T(8,128)(2,1)} %value_own.5, bf16[320,5120]{1,0:T(8,128)(2,1)} %copy-done.6, ...), custom_call_target="tpu_custom_call", output_to_operand_aliasing={{}: (6, {})} | custom-call | flops 1572864000 | bytes 4915200 | tf_op jit(solution)/shard_map/spatial_heads/pallas_call | solution.py:114
  251.0 0.0 collective-permute-done.10.far
  251.0 0.8 copy-done.12
  251.7 26.6 %finish.1 = bf16[320,5120]{1,0:T(8,128)(2,1)} custom-call(s32[120]{0:T(128)} %get-tuple-element.12.meta, s32[3]{0:T(128)} %pad_add_fusion.place, bf16[10,160,128]{2,1,0:T(8,128)(2,1)} %copy-done.3, bf16[10,160,128]{2,1,0:T(8,128)(2,1)} %copy-done.12, bf16[320,5120]{1,0:T(8,128)(2,1)} %spatial_heads.5.so_far), custom_call_target="tpu_custom_call", output_to_operand_aliasing={{}: (4, {})} | custom-call | bytes 1638400 | tf_op jit(solution)/shard_map/finish/pallas_call | solution.py:216
  (11 shorter events, 0.0 us)
Async XLA Ops:
  0.0 188.4 %collective-permute-start.11 = (bf16[320,5120]{1,0:T(8,128)(2,1)}, bf16[320,5120]{1,0:T(8,128)(2,1)S(1)}, u32[]{:S(2)}, u32[]{:S(2)}) collective-permute-start(bf16[320,5120]{1,0:T(8,128)(2,1)} %key_own.5), channel_id=1, source_target_pairs={{0,1},{1,0},{2,3},{3,2},{4,5},{5,4},{6,7},{7,6},{8,9},{9,8},{10,11... | collective-permute-start | bytes 9830408 | tf_op jit(solution)/shard_map/ppermute | solution.py:21
  0.5 188.0 %collective-permute-start.12 = (bf16[320,5120]{1,0:T(8,128)(2,1)}, bf16[320,5120]{1,0:T(8,128)(2,1)}, u32[]{:S(2)}, u32[]{:S(2)}) collective-permute-start(bf16[320,5120]{1,0:T(8,128)(2,1)} %value_own.5), channel_id=1, source_target_pairs={{0,1},{1,0},{2,3},{3,2},{4,5},{5,4},{6,7},{7,6},{8,9},{9,8},{10,11... | collective-permute-start | bytes 9830408 | tf_op jit(solution)/shard_map/ppermute | solution.py:21
  1.1 166.6 %copy-start.5 = (s32[3]{0:T(128)S(1)}, s32[3]{0:T(128)}, u32[]{:S(2)}) copy-start(s32[3]{0:T(128)} %pad_add_fusion.place) | copy-start | bytes 40
  78.0 13.5 %collective-permute-start = (bf16[10,160,128]{2,1,0:T(8,128)(2,1)}, bf16[10,160,128]{2,1,0:T(8,128)(2,1)S(1)}, u32[]{:S(2)}, u32[]{:S(2)}) collective-permute-start(bf16[10,160,128]{2,1,0:T(8,128)(2,1)} %get-tuple-element.14), channel_id=1, source_target_pairs={{0,2},{1,3},{2,0},{3,1},{4,6},{5,7},{6,4},{7,5},{8,10},{9,11},{10,... | collective-permute-start | bytes 1228808 | tf_op jit(solution)/shard_map/ppermute | solution.py:21
  81.0 27.4 %collective-permute-start.1 = (bf16[2,10,160,128]{3,2,1,0:T(8,128)(2,1)}, bf16[2,10,160,128]{3,2,1,0:T(8,128)(2,1)S(1)}, u32[]{:S(2)}, u32[]{:S(2)}) collective-permute-start(bf16[2,10,160,128]{3,2,1,0:T(8,128)(2,1)} %get-tuple-element.16), channel_id=1, source_target_pairs={{0,2},{1,3},{2,0},{3,1},{4,6},{5,7},{6,4},{7,5},{8,10},{9,11},{10,... | collective-permute-start | bytes 2457608 | tf_op jit(solution)/shard_map/ppermute | solution.py:21
  81.1 28.6 %collective-permute-start.4 = (bf16[2,10,160,128]{3,2,1,0:T(8,128)(2,1)}, bf16[2,10,160,128]{3,2,1,0:T(8,128)(2,1)S(1)}, u32[]{:S(2)}, u32[]{:S(2)}) collective-permute-start(bf16[2,10,160,128]{3,2,1,0:T(8,128)(2,1)} %get-tuple-element.15.rest_0_), channel_id=1, source_target_pairs={{4,0},{5,1},{6,2},{7,3},{8,4},{9,5},{10,6},{11,7},{12,8},{13,9},{1... | collective-permute-start | bytes 2457608 | tf_op jit(solution)/shard_map/ppermute | solution.py:27
  91.5 22.8 %collective-permute-start.2 = (bf16[2,10,160,128]{3,2,1,0:T(8,128)(2,1)}, bf16[2,10,160,128]{3,2,1,0:T(8,128)(2,1)S(1)}, u32[]{:S(2)}, u32[]{:S(2)}) collective-permute-start(bf16[2,10,160,128]{3,2,1,0:T(8,128)(2,1)} %get-tuple-element.15.rest_0_), channel_id=1, source_target_pairs={{0,4},{1,5},{2,6},{3,7},{4,8},{5,9},{6,10},{7,11},{8,12},{9,13},{1... | collective-permute-start | bytes 2457608 | tf_op jit(solution)/shard_map/ppermute | solution.py:27
  108.4 23.1 %collective-permute-start.5 = (bf16[2,10,160,128]{3,2,1,0:T(8,128)(2,1)S(1)}, bf16[2,10,160,128]{3,2,1,0:T(8,128)(2,1)S(1)}, u32[]{:S(2)}, u32[]{:S(2)}) collective-permute-start(bf16[2,10,160,128]{3,2,1,0:T(8,128)(2,1)S(1)} %collective-permute-done.1.rest_1_), channel_id=1, source_target_pairs={{4,0},{5,1},{6,2},{7,3},{8,4},{9,5},{10,6},{11,7},{12,8},{13,9},{1... | collective-permute-start | bytes 2457608 | tf_op jit(solution)/shard_map/ppermute | solution.py:27
  109.7 25.5 %collective-permute-start.3 = (bf16[2,10,160,128]{3,2,1,0:T(8,128)(2,1)S(1)}, bf16[2,10,160,128]{3,2,1,0:T(8,128)(2,1)S(1)}, u32[]{:S(2)}, u32[]{:S(2)}) collective-permute-start(bf16[2,10,160,128]{3,2,1,0:T(8,128)(2,1)S(1)} %collective-permute-done.1.rest_1_), channel_id=1, source_target_pairs={{0,4},{1,5},{2,6},{3,7},{4,8},{5,9},{6,10},{7,11},{8,12},{9,13},{1... | collective-permute-start | bytes 2457608 | tf_op jit(solution)/shard_map/ppermute | solution.py:27
  114.3 34.7 %collective-permute-start.8 = (bf16[2,10,160,128]{3,2,1,0:T(8,128)(2,1)S(1)}, bf16[2,10,160,128]{3,2,1,0:T(8,128)(2,1)S(1)}, u32[]{:S(2)}, u32[]{:S(2)}) collective-permute-start(bf16[2,10,160,128]{3,2,1,0:T(8,128)(2,1)S(1)} %collective-permute-done.4.rest_4_), channel_id=1, source_target_pairs={{4,0},{5,1},{6,2},{7,3},{8,4},{9,5},{10,6},{11,7},{12,8},{13,9},{1... | collective-permute-start | bytes 2457608 | tf_op jit(solution)/shard_map/ppermute | solution.py:27
  131.5 35.3 %copy-start.7 = (bf16[2,10,160,128]{3,2,1,0:T(8,128)(2,1)}, bf16[2,10,160,128]{3,2,1,0:T(8,128)(2,1)S(1)}, u32[]{:S(2)}) copy-start(bf16[2,10,160,128]{3,2,1,0:T(8,128)(2,1)S(1)} %collective-permute-done.5.rest_5_) | copy-start | bytes 2457604
  131.5 21.3 %collective-permute-start.6 = (bf16[2,10,160,128]{3,2,1,0:T(8,128)(2,1)S(1)}, bf16[2,10,160,128]{3,2,1,0:T(8,128)(2,1)S(1)}, u32[]{:S(2)}, u32[]{:S(2)}) collective-permute-start(bf16[2,10,160,128]{3,2,1,0:T(8,128)(2,1)S(1)} %collective-permute-done.2.rest_2_), channel_id=1, source_target_pairs={{0,4},{1,5},{2,6},{3,7},{4,8},{5,9},{6,10},{7,11},{8,12},{9,13},{1... | collective-permute-start | bytes 2457608 | tf_op jit(solution)/shard_map/ppermute | solution.py:27
  135.3 29.8 %collective-permute-start.9 = (bf16[2,10,160,128]{3,2,1,0:T(8,128)(2,1)S(1)}, bf16[2,10,160,128]{3,2,1,0:T(8,128)(2,1)S(1)}, u32[]{:S(2)}, u32[]{:S(2)}) collective-permute-start(bf16[2,10,160,128]{3,2,1,0:T(8,128)(2,1)S(1)} %collective-permute-done.5.rest_5_), channel_id=1, source_target_pairs={{4,0},{5,1},{6,2},{7,3},{8,4},{9,5},{10,6},{11,7},{12,8},{13,9},{1... | collective-permute-start | bytes 2457608 | tf_op jit(solution)/shard_map/ppermute | solution.py:27
  149.1 17.7 %copy-start.8 = (bf16[2,10,160,128]{3,2,1,0:T(8,128)(2,1)}, bf16[2,10,160,128]{3,2,1,0:T(8,128)(2,1)S(1)}, u32[]{:S(2)}) copy-start(bf16[2,10,160,128]{3,2,1,0:T(8,128)(2,1)S(1)} %collective-permute-done.8.rest_8_) | copy-start | bytes 2457604
  149.1 17.7 %collective-permute-start.7 = (bf16[2,10,160,128]{3,2,1,0:T(8,128)(2,1)S(1)}, bf16[2,10,160,128]{3,2,1,0:T(8,128)(2,1)S(1)}, u32[]{:S(2)}, u32[]{:S(2)}) collective-permute-start(bf16[2,10,160,128]{3,2,1,0:T(8,128)(2,1)S(1)} %collective-permute-done.3.rest_3_), channel_id=1, source_target_pairs={{0,4},{1,5},{2,6},{3,7},{4,8},{5,9},{6,10},{7,11},{8,12},{9,13},{1... | collective-permute-start | bytes 2457608 | tf_op jit(solution)/shard_map/ppermute | solution.py:27
  152.8 13.9 %copy-start.9 = (bf16[2,10,160,128]{3,2,1,0:T(8,128)(2,1)}, bf16[2,10,160,128]{3,2,1,0:T(8,128)(2,1)S(1)}, u32[]{:S(2)}) copy-start(bf16[2,10,160,128]{3,2,1,0:T(8,128)(2,1)S(1)} %collective-permute-done.6.rest_6_) | copy-start | bytes 2457604
  165.0 1.7 copy-start.10
  166.7 0.9 copy-start.11
  167.7 1.1 copy-start.1
  168.8 1.0 copy-start.2
  169.8 0.6 copy-start.4
  170.4 19.8 %copy-start = (bf16[320,5120]{1,0:T(8,128)(2,1)S(1)}, bf16[320,5120]{1,0:T(8,128)(2,1)}, u32[]{:S(2)}) copy-start(bf16[320,5120]{1,0:T(8,128)(2,1)} %query.5) | copy-start | bytes 9830404
  186.8 23.6 %copy-start.3 = (bf16[10,160,128]{2,1,0:T(8,128)(2,1)}, bf16[10,160,128]{2,1,0:T(8,128)(2,1)S(1)}, u32[]{:S(2)}) copy-start(bf16[10,160,128]{2,1,0:T(8,128)(2,1)S(1)} %get-tuple-element.17.own) | copy-start | bytes 1228804
  186.9 64.1 %collective-permute-start.10 = (bf16[10,160,128]{2,1,0:T(8,128)(2,1)S(1)}, bf16[10,160,128]{2,1,0:T(8,128)(2,1)S(1)}, u32[]{:S(2)}, u32[]{:S(2)}) collective-permute-start(bf16[10,160,128]{2,1,0:T(8,128)(2,1)S(1)} %get-tuple-element.18), channel_id=1, source_target_pairs={{0,2},{1,3},{2,0},{3,1},{4,6},{5,7},{6,4},{7,5},{8,10},{9,11},{10,... | collective-permute-start | bytes 1228808 | tf_op jit(solution)/shard_map/ppermute | solution.py:21
  188.4 1.7 copy-start.6
  251.0 0.8 copy-start.12
